TPU v7x, 256 devices: a whole 4x4x8 slice. The times are simulated.
256 devices in a mesh: dap: 64 (over x, y_hi, z), rep: 4 (over y_lo, core).
Axes of the slice: x: 4, y: 4 (y_hi: 2, y_lo: 2; y = y_hi * 2 + y_lo), z: 8, core: 2. Of those that a mesh axis runs over, the one named last changes fastest.
Arguments:
- pair: bfloat16 [2048, 512, 128], P(('rep', 'dap')), parts along dimension 0, may hold values from -100 to 100
- pair_mask: int32 [2048, 512], P(('rep', 'dap')), parts along dimension 0, may hold values 0 or 1
- chain_ids: int32 [2048], P('rep'), parts along dimension 0, may hold values from 0 to 3, never falling along the last dimension, each value on 1 to 256 neighbouring positions
- norm_gain: float32 [3, 128], replicated, may hold values from 0.5 to 1.5
- norm_shift: float32 [3, 128], replicated, may hold values from -3 to 3
- attn_proj: bfloat16 [2, 128, 512], replicated, may hold values from -1 to 1
- gate_shift: float32 [2, 128], replicated, may hold values from -4 to 4
- bias_proj: bfloat16 [2, 128, 4], replicated, may hold values from -4 to 4
- chain_scale: float32 [2, 4], replicated, may hold values from -2 to 250
- attn_out: bfloat16 [2, 128, 128], replicated, may hold values from -0.5 to 0.5
- trans_in: bfloat16 [128, 512], replicated, may hold values from -0.5 to 0.5
- trans_out: bfloat16 [512, 128], replicated, may hold values from -0.25 to 0.25
Outputs:
- updated: bfloat16 [2048, 512, 128], P(('rep', 'dap')), parts along dimension 0
There are 4 independent parts, one for each index of `rep`. A program takes and returns all parts, laid end to end along the dimension named above; an argument that names none is the same for every part. Nothing has to cross between parts.
Inputs may be any that keep to these rules, and one draw needn't show every extreme that they name: `chain_ids`: never falls along the residues.
All inputs are finite; a program needn't handle non-finite values. No bound on the sum of `pair_mask` on one device may be relied on, other than what follows from the above.
Results may differ from a plain program's by a relative error of at most 0.02.
Values may be sent and summed in bfloat16 or wider, within the bound.
A program may use at most 64 MiB of HBM per device.

v0:
```python
import jax
import jax.numpy as jnp
from jax import lax
from jax.sharding import PartitionSpec as P


def normalize(x, gain, shift):
    mean = jnp.mean(x, axis=-1, keepdims=True)
    center = x - mean
    var = jnp.mean(center * center, axis=-1, keepdims=True)
    return center * lax.rsqrt(var + 1e-05) * gain + shift


def attend_block(x_row, query, keys, values, gate, bias, extra, mask_row, w_out):
    scores = jnp.einsum("jhd,khd->hjk", query, keys, preferred_element_type=jnp.float32)
    logits = scores + bias + extra + mask_row[None, None, :]
    top = jnp.max(logits, axis=-1, keepdims=True)
    expd = jnp.exp(logits - top)
    weights = (expd / jnp.sum(expd, axis=-1, keepdims=True)).astype(jnp.bfloat16)
    mixed = jnp.einsum("hjk,khd->jhd", weights, values, preferred_element_type=jnp.float32)
    width = query.shape[1] * query.shape[2]
    gated = (mixed * gate).astype(jnp.bfloat16).reshape(query.shape[0], width)
    return (x_row + jnp.dot(gated, w_out, preferred_element_type=jnp.float32)).astype(jnp.bfloat16)


def attend_rows(x, query, keys, values, gate, bias, extra, mask_term, w_out):

    def one_row(items):
        x_row, q_row, k_row, v_row, g_row, m_row = items
        return attend_block(x_row, q_row, k_row, v_row, g_row, bias, extra, m_row, w_out)

    return lax.map(one_row, (x, query, keys, values, gate, mask_term))


def triangle(
    pair_rows,
    mask_rows,
    chain_ids,
    layer,
    norm_gain,
    norm_shift,
    attn_proj,
    gate_shift,
    bias_proj,
    chain_scale,
    attn_out,
):
    hidden = gate_shift.shape[1]
    heads = bias_proj.shape[2]
    head_dim = hidden // heads
    x = pair_rows.astype(jnp.float32)
    normed = normalize(x, norm_gain[layer], norm_shift[layer]).astype(jnp.bfloat16)
    proj = jnp.einsum("rnc,cf->rnf", normed, attn_proj[layer], preferred_element_type=jnp.float32)
    shape = proj.shape[:2] + (heads, head_dim)
    query = (proj[..., :hidden] * head_dim ** (-0.5)).astype(jnp.bfloat16).reshape(shape)
    keys = proj[..., hidden : 2 * hidden].astype(jnp.bfloat16).reshape(shape)
    values = proj[..., 2 * hidden : 3 * hidden].astype(jnp.bfloat16).reshape(shape)
    gate = jax.nn.sigmoid(proj[..., 3 * hidden :] + gate_shift[layer]).reshape(shape)
    planes = jnp.einsum("rnc,ch->hrn", normed, bias_proj[layer], preferred_element_type=jnp.float32)
    same = (chain_ids[:, None] == chain_ids[None, :]).astype(jnp.float32)
    extra = chain_scale[layer][:, None, None] * same[None]
    mask_term = (mask_rows.astype(jnp.float32) - 1.0) * 1000000000.0
    w_out = attn_out[layer]
    full_bias = lax.all_gather(planes.astype(jnp.bfloat16), "dap", axis=1, tiled=True).astype(
        planes.dtype
    )
    result = attend_rows(x, query, keys, values, gate, full_bias, extra, mask_term, w_out)
    return result


def transition(pair_rows, norm_gain, norm_shift, trans_in, trans_out):
    y = pair_rows.astype(jnp.float32)
    normed = normalize(y, norm_gain[2], norm_shift[2]).astype(jnp.bfloat16)
    inner = jax.nn.relu(
        jnp.einsum("rnc,cf->rnf", normed, trans_in, preferred_element_type=jnp.float32)
    ).astype(jnp.bfloat16)
    return (
        y + jnp.einsum("rnf,fc->rnc", inner, trans_out, preferred_element_type=jnp.float32)
    ).astype(jnp.bfloat16)


def body(
    pair,
    pair_mask,
    chain_ids,
    norm_gain,
    norm_shift,
    attn_proj,
    gate_shift,
    bias_proj,
    chain_scale,
    attn_out,
    trans_in,
    trans_out,
):
    params = (norm_gain, norm_shift, attn_proj, gate_shift, bias_proj, chain_scale, attn_out)
    start = triangle(pair, pair_mask, chain_ids, 0, *params)
    swapped = jnp.swapaxes(start, 0, 1)
    mask_swapped = jnp.swapaxes(pair_mask, 0, 1)
    columns, mask_columns = (
        lax.all_to_all(swapped, "dap", split_axis=0, concat_axis=1, tiled=True),
        lax.all_to_all(mask_swapped, "dap", split_axis=0, concat_axis=1, tiled=True),
    )
    ending = triangle(columns, mask_columns, chain_ids, 1, *params)
    restored = lax.all_to_all(
        jnp.swapaxes(ending, 0, 1), "dap", split_axis=0, concat_axis=1, tiled=True
    )
    restored = transition(restored, norm_gain, norm_shift, trans_in, trans_out)
    return restored


def solution(mesh):
    in_specs = (
        P(("rep", "dap"), None, None),
        P(("rep", "dap"), None),
        P("rep"),
        P(),
        P(),
        P(),
        P(),
        P(),
        P(),
        P(),
        P(),
        P(),
    )
    out_specs = P(("rep", "dap"), None, None)
    return jax.shard_map(body, mesh=mesh, in_specs=in_specs, out_specs=out_specs, check_vma=False)
```

profile of v0, /device:TPU:2, one launch (start us, length us, event | category | flops | bytes accessed | tf_op | source)
XLA Modules:
  0.0 528.6 jit_solution(15407953299674974178)
XLA Ops:
  19.7 113.9 %all-gather.3.cloned.1.call-done = bf16[4,512,512]{2,0,1:T(4,128)(2,1)} async-done(((bf16[4,8,512]{2,0,1:T(4,128)(2,1)}), bf16[4,512,512]{2,0,1:T(4,128)(2,1)}) %all-gather.3.cloned.1.call-update) | async-done | bytes 2097168 | tf_op jit(solution)/shard_map/all_gather | solution.py:64
  133.5 4.8 copy.131
  138.5 89.3 %while.22 = (s32[]{:T(128)}, bf16[8,512,128]{2,1,0:T(8,128)(2,1)S(1)}, f32[8,512,128]{2,1,0:T(8,128)}, bf16[8,512,4,32]{1,3,2,0:T(8,128)(2,1)}, bf16[8,512,4,32]...) while((s32[]{:T(128)}, ...), condition=%wide.region_5.6_spmd.clone, body=%wide.region_2.5_spmd.clone.sunk | while | flops 160697344 | bytes 40166056 | solution.py:32
  143.9 4.6 fusion.137
  149.7 3.4 fusion.135
  155.0 4.6 fusion.137
  160.9 3.4 fusion.135
  166.2 4.6 fusion.137
  172.0 3.4 fusion.135
  177.4 4.6 fusion.137
  183.2 3.4 fusion.135
  188.5 4.6 fusion.137
  194.4 3.4 fusion.135
  199.7 4.6 fusion.137
  210.9 4.6 fusion.137
  216.7 3.4 fusion.135
  222.0 4.6 fusion.137
  228.5 33.9 %all_to_all.31 = bf16[512,8,128]{2,1,0:T(8,128)(2,1)S(1)} all-to-all(bf16[512,8,128]{2,1,0:T(8,128)(2,1)S(1)} %bitcast.248), channel_id=1, replica_groups=mesh['dap'=64,'rep'=4] {'dap'}, dimensions={0} | all-to-all | bytes 2097152 | tf_op jit(solution)/shard_map/all_to_all | solution.py:101
  267.4 18.4 %all_to_all.32 = s32[64,8,8]{1,2,0:T(8,128)S(1)} all-to-all(s32[64,8,8]{1,2,0:T(8,128)S(1)} %copy.140), channel_id=1, replica_groups=mesh['dap'=64,'rep'=4] {'dap'}, dimensions={0} | all-to-all | bytes 32768 | tf_op jit(solution)/shard_map/all_to_all | solution.py:102
  293.7 87.5 %all-gather.5.cloned.1.call-done = bf16[4,512,512]{2,0,1:T(4,128)(2,1)} async-done(((bf16[4,8,512]{2,0,1:T(4,128)(2,1)}), bf16[4,512,512]{2,0,1:T(4,128)(2,1)}) %all-gather.5.cloned.1.call-update) | async-done | bytes 2097168 | tf_op jit(solution)/shard_map/all_gather | solution.py:64
  381.2 4.8 copy.143
  386.1 89.3 %while.23 = (s32[]{:T(128)}, bf16[8,512,128]{2,1,0:T(8,128)(2,1)S(1)}, f32[8,512,128]{2,1,0:T(8,128)}, bf16[8,512,4,32]{1,3,2,0:T(8,128)(2,1)}, bf16[8,512,4,32]...) while((s32[]{:T(128)}, ...), condition=%wide.region_11.12_spmd.clone, body=%wide.region_8.11_spmd.clone.sunk | while | flops 160697344 | bytes 40166056 | solution.py:32
  391.5 4.6 fusion.148
  402.7 4.6 fusion.148
  413.8 4.6 fusion.148
  425.0 4.6 fusion.148
  436.2 4.6 fusion.148
  447.3 4.6 fusion.148
  458.5 4.6 fusion.148
  469.7 4.6 fusion.148
  476.2 33.9 %all_to_all.33 = bf16[512,8,128]{2,1,0:T(8,128)(2,1)S(1)} all-to-all(bf16[512,8,128]{2,1,0:T(8,128)(2,1)S(1)} %bitcast.249), channel_id=1, replica_groups=mesh['dap'=64,'rep'=4] {'dap'}, dimensions={0} | all-to-all | bytes 2097152 | tf_op jit(solution)/shard_map/all_to_all | solution.py:105
  517.5 4.3 fusion.58
  (165 shorter events, 118.7 us)
Async XLA Ops:
  6.5 511.0 %copy-start = (bf16[512,128]{1,0:T(8,128)(2,1)S(1)}, bf16[512,128]{1,0:T(8,128)(2,1)}, u32[]{:S(2)}) copy-start(bf16[512,128]{1,0:T(8,128)(2,1)} %param.27) | copy-start | bytes 393220
  6.5 4.1 copy-start.3
  6.5 4.1 copy-start.8
  6.5 4.1 copy-start.9
  6.5 4.1 copy-start.12
  6.5 127.0 %all-gather.3.cloned.1.call-start = ((), (), s32[]{:S(2)}) async-start(), calls=%async_computation.3 | async-start | bytes 2129920 | tf_op jit(solution)/shard_map/all_gather | solution.py:64
  12.8 1.6 copy-start.10
  12.8 1.7 copy-start.11
  12.8 1.7 copy-start.5
  12.8 1.7 copy-start.6
  12.8 1.7 copy-start.7
  12.8 1.8 copy-start.4
  12.8 368.3 %all-gather.5.cloned.1.call-start = ((), (), s32[]{:S(2)}) async-start(), calls=%async_computation.4 | async-start | bytes 2129920 | tf_op jit(solution)/shard_map/all_gather | solution.py:64
  141.9 2.0 copy-start.1
  153.1 2.0 copy-start.1
  164.2 2.0 copy-start.1
  175.4 2.0 copy-start.1
  186.6 2.0 copy-start.1
  197.7 2.0 copy-start.1
  208.9 2.0 copy-start.1
  220.1 2.0 copy-start.1
  389.5 2.0 copy-start.2
  400.7 2.0 copy-start.2
  411.9 2.0 copy-start.2
  423.0 2.0 copy-start.2
  434.2 2.0 copy-start.2
  445.4 2.0 copy-start.2
  456.5 2.0 copy-start.2
  467.7 2.0 copy-start.2
Sparse Core Ops, SparseCore 0:
  12.9 120.5 all-gather.2
  267.2 113.8 all-gather.4
where the time goes:
time: 531 us; the launch traced here: 529 us
  waiting for transfers between devices  201 us (38%)
  matrix products  159 us (30%)
  blocking collectives  86.3 us (16%)
  local copies, waits for them, and re-layouts  36.6 us (7%)
  other arithmetic  31.1 us (6%)
  between operations  13.7 us (3%)
    all_gather x2, waiting for transfers between devices, triangle(): lax.all_gather(planes.astype(jnp.bfloat16), 'dap', axis=1, tiled=True)  201 us
    dot_general x16, matrix products, attend_block(): jnp.einsum('hjk,khd->jhd', weights, values, preferred_element_type=jnp.fl...  73.6 us
    dot_general x16, matrix products, attend_block(): jnp.einsum('jhd,khd->hjk', query, keys, preferred_element_type=jnp.float32)  53.6 us
    all_to_all x1, blocking collectives, body(): lax.all_to_all(jnp.swapaxes(ending, 0, 1), 'dap', split_axis=0, concat_ax...  33.9 us
    all_to_all x1, blocking collectives, body(): lax.all_to_all(swapped, 'dap', split_axis=0, concat_axis=1, tiled=True)  33.9 us
    dot_general x16, matrix products, attend_block(): jnp.dot(gated, w_out, preferred_element_type=jnp.float32)  19 us
    while x32, local copies, waits for them, and re-layouts  18.4 us
    all_to_all x1, blocking collectives, body(): lax.all_to_all(mask_swapped, 'dap', split_axis=0, concat_axis=1, tiled=True)  18.4 us
  transfers between devices with their start and end apart: 2, of which 2 were waited for; matrix products, arithmetic and copies ran while one was open for 3% of the time, Pallas kernels for 0%

commit v1 on v0

v1 whole, which is shorter than its diff:
```python
import functools

import jax
import jax.numpy as jnp
from jax import lax
from jax.experimental import pallas as pl
from jax.experimental.pallas import tpu as pltpu
from jax.sharding import PartitionSpec as P

C = 128
HEADS = 4
DX = (0, 0, 2, 1, 3, 1, 3, 2)
DY = (0, 1, 0, 0, 0, 1, 1, 1)
F32 = jnp.float32
BF16 = jnp.bfloat16
NT = (((1,), (1,)), ((), ()))


def layer_norm(x, gain, shift):
    mean = jnp.mean(x, axis=-1, keepdims=True)
    center = x - mean
    var = jnp.mean(center * center, axis=-1, keepdims=True)
    return center * lax.rsqrt(var + 1e-05) * gain + shift


def pick(t, table):
    value = jnp.int32(table[0])
    for index in range(1, len(table)):
        value = jnp.where(t == index, jnp.int32(table[index]), value)
    return value


def kernel(
    nz,
    pair,
    mask,
    cid,
    gain,
    shift,
    wp,
    gsh,
    bp,
    wo,
    ti,
    to,
    scale,
    out,
    xs,
    xt,
    xn,
    q,
    k,
    vo,
    gate,
    bt,
    bx,
    gs,
    mrow,
    cidc,
    mz,
    mt,
    mrecv,
    planes,
    stage,
    recv,
    z_send,
    z_recv,
    p_send,
    p_recv,
    a_send,
    a_recv,
    m_send,
    m_recv,
    l_sem,
):
    n = pair.shape[1]
    nd = 8 * nz
    rows = 8 * nz
    group = 128 // rows
    me = lax.axis_index("dap")
    z = lax.rem(me, nz)
    pm = lax.div(me, nz)
    xx = lax.div(pm, 2)
    yy = lax.rem(pm, 2)

    def plane(dx, dy):
        return lax.rem(xx + dx, 4) * 2 + lax.rem(yy + dy, 2)

    def send(src, dst, send_sem, recv_sem, dest):
        pltpu.make_async_remote_copy(
            src_ref=src,
            dst_ref=dst,
            send_sem=send_sem,
            recv_sem=recv_sem,
            device_id={"dap": dest},
            device_id_type=pl.DeviceIdType.MESH,
        ).start()

    def drain(ref, sem):
        pltpu.make_async_copy(ref, ref, sem).wait()

    mz[...] = jnp.zeros_like(mz)
    barrier = pltpu.get_barrier_semaphore()

    def greet(d, carry):
        pl.semaphore_signal(
            barrier,
            inc=1,
            device_id={"dap": lax.rem(me + d, nd)},
            device_id_type=pl.DeviceIdType.MESH,
        )
        return carry

    lax.fori_loop(1, nd, greet, 0)

    lane_head = lax.div(lax.broadcasted_iota(jnp.int32, (1, 1, C), 2), 32)
    cid_row = cid[...].astype(F32)
    cidc[...] = jnp.transpose(jnp.broadcast_to(cid_row, (128, n)))
    mask_f = mask[...].astype(F32)
    mrow[0] = (mask_f - 1.0) * 1e9
    ones = jnp.ones((n, C), BF16)
    for r in range(8):
        vo[r, :, C:] = ones

    for layer in range(2):
        g_l, s_l = gain[layer : layer + 1, :], shift[layer : layer + 1, :]
        if layer == 1:
            def unpack(s, carry):
                xt[pl.ds(pl.multiple_of(s * 64, 64), 64), :] = recv[0, s].astype(F32)
                return carry

            lax.fori_loop(0, nd, unpack, 0, unroll=8)

        def norm_row(r, carry):
            if layer == 0:
                x = pair[r].astype(F32)
            else:
                x = xt[pl.ds(r, n, stride=8), :]
            xs[r] = x
            xnv = layer_norm(x, g_l, s_l).astype(BF16)
            xn[r] = xnv
            b = lax.dot_general(bp[layer], xnv, NT, preferred_element_type=F32)
            for c in range(n // 128):
                bt[c, pl.ds(pl.multiple_of(r * 8, 8), 4), :] = b[:, c * 128 : (c + 1) * 128]
            return carry

        lax.fori_loop(0, 8, norm_row, 0)
        for c in range(n // 128):
            own = [bt[c, pl.ds(h, 8, stride=8), :] for h in range(HEADS)]
            own = jnp.concatenate(own, axis=0).astype(BF16)
            planes[layer, pm, z, :, c * 128 : (c + 1) * 128] = own

        if layer == 0:
            pl.semaphore_wait(barrier, nd - 1)
        for d in range(1, nz):
            ref = planes.at[layer, pm, z]
            send(ref, ref, z_send.at[layer], z_recv.at[layer], pm * nz + lax.rem(z + d, nz))
        if layer == 0:
            at = pl.ds(pl.multiple_of(lax.rem(pm, group) * rows + z * 8, 8), 8)
            mz[at, :] = mask_f
            for d in range(1, nz):
                ref = mz.at[at, :]
                send(ref, ref, m_send.at[0], m_recv.at[0], pm * nz + lax.rem(z + d, nz))

        gate_shift = gsh[layer : layer + 1, :]

        def project(r, carry):
            f = jnp.dot(xn[r], wp[layer], preferred_element_type=F32)
            q[r] = f[:, :C] * (32 ** -0.5)
            k[r] = f[:, C : 2 * C].astype(BF16)
            vo[r, :, :C] = f[:, 2 * C : 3 * C].astype(BF16)
            gate[r] = jax.nn.sigmoid(f[:, 3 * C :] + gate_shift)
            return carry

        lax.fori_loop(0, 8, project, 0)

        drain(planes.at[layer, pm, pl.ds(0, nz - 1)], z_recv.at[layer])
        for dx, dy in ((0, 1), (2, 0), (1, 0), (3, 0)):
            ref = planes.at[layer, pm]
            send(ref, ref, p_send.at[layer], p_recv.at[layer, pm], plane(dx, dy) * nz + z)
        if layer == 0:
            drain(mz.at[pl.ds(0, (nz - 1) * 8)], m_recv.at[0])
            mt[...] = jnp.transpose(mz[...])
            for t in range(1, 8):
                pt = plane(DX[t], DY[t])
                src = mt.at[pl.ds(pl.multiple_of((pt * nz + z) * 8, 8), 8), :]
                send(src, mrecv.at[pm], m_send.at[1], m_recv.at[1], pt * nz + z)
            mrecv[pm] = mt[pl.ds(pl.multiple_of(me * 8, 8), 8), :]

        def block(t, carry):
            m = plane(pick(t, DX), pick(t, DY))

            @pl.when(t > 0)
            def _():
                drain(planes.at[layer, m], p_recv.at[layer, m])

            @pl.when(t == 1)
            def _():
                for dx in (1, 3):
                    ref = planes.at[layer, m]
                    send(ref, ref, p_send.at[layer], p_recv.at[layer, m], plane(dx, 0) * nz + z)

            @pl.when(t == 2)
            def _():
                ref = planes.at[layer, m]
                send(ref, ref, p_send.at[layer], p_recv.at[layer, m], plane(0, 1) * nz + z)

            here = pl.ds(pl.multiple_of(m * rows, rows), rows)
            cb = cidc[here, :]
            for c in range(n // 128):
                lanes = slice(c * 128, (c + 1) * 128)
                same = jnp.where(cb == cid_row[:, lanes], 1.0, 0.0).reshape(nz, 8, 128)
                b = planes[layer, m, :, :, lanes].astype(F32).reshape(nz, HEADS, 8, 128)
                b = jnp.stack(
                    [b[:, h] + scale[layer, h] * same for h in range(HEADS)], axis=1
                )
                bx[:, lanes] = b.reshape(4 * rows, 128)

            for i in range(8):
                qi = q[i, here, :].reshape(nz, 8, C)
                qm = jnp.stack(
                    [jnp.where(lane_head == h, qi, 0.0) for h in range(HEADS)], axis=1
                )
                qm = qm.reshape(4 * rows, C).astype(BF16)
                s = lax.dot_general(qm, k[i], NT, preferred_element_type=F32)
                s = s + bx[...] + mrow[layer, i : i + 1, :]
                top = jnp.max(s, axis=-1, keepdims=True)
                p = jnp.exp(s - top).astype(BF16)
                o = jnp.dot(p, vo[i], preferred_element_type=F32)
                o = o.reshape(nz, HEADS, 8, 2 * C)
                mixed, total = o[:, 0, :, :C], o[:, 0, :, C:]
                for h in range(1, HEADS):
                    mixed = jnp.where(lane_head == h, o[:, h, :, :C], mixed)
                    total = jnp.where(lane_head == h, o[:, h, :, C:], total)
                weighted = (mixed / total).reshape(rows, C) * gate[i, here, :]
                gs[i * rows : (i + 1) * rows, :] = weighted.astype(BF16)

            y = jnp.dot(gs[...], wo[layer], preferred_element_type=F32)
            y = y + xs[:, here, :].reshape(8 * rows, C)
            if layer == 1:
                y = y.astype(BF16).astype(F32)
                yn = layer_norm(y, gain[2:3, :], shift[2:3, :]).astype(BF16)
                inner = jnp.dot(yn, ti[...], preferred_element_type=F32)
                inner = jnp.maximum(inner, 0.0).astype(BF16)
                y = y + jnp.dot(inner, to[...], preferred_element_type=F32)
            y = y.reshape(8, nz, 8, C)
            for zz in range(nz):
                stage[layer, m, zz] = y[:, zz].reshape(64, C).astype(BF16)

            for d in range(nz):
                zt = lax.rem(z + d, nz)

                def go(zt=zt):
                    send(
                        stage.at[layer, m, zt],
                        recv.at[layer, me],
                        a_send.at[layer],
                        a_recv.at[layer],
                        m * nz + zt,
                    )

                if d == 0:
                    pl.when(t > 0)(go)

                    @pl.when(t == 0)
                    def _():
                        copy = pltpu.make_async_copy(
                            stage.at[layer, m, z], recv.at[layer, me], l_sem
                        )
                        copy.start()
                        copy.wait()
                else:
                    go()
            return carry

        lax.fori_loop(0, 8, block, 0)

        if layer == 0:
            drain(mrecv.at[pl.ds(0, 7)], m_recv.at[1])
            parts = []
            for c in range(n // 128):
                part = mrecv[c * group]
                for g in range(1, group):
                    part = part + mrecv[c * group + g]
                parts.append(part)
            mrow[1] = (jnp.concatenate(parts, axis=1) - 1.0) * 1e9
        drain(recv.at[layer, pl.ds(0, nd - 1)], a_recv.at[layer])

    def unpack_last(s, carry):
        xt[pl.ds(pl.multiple_of(s * 64, 64), 64), :] = recv[1, s].astype(F32)
        return carry

    lax.fori_loop(0, nd, unpack_last, 0, unroll=8)
    for r in range(8):
        out[r] = xt[pl.ds(r, n, stride=8), :].astype(BF16)

    for layer in range(2):
        drain(planes.at[layer, 0, pl.ds(0, nz - 1)], z_send.at[layer])
        drain(planes.at[layer, pl.ds(0, 7)], p_send.at[layer])
        drain(recv.at[layer, pl.ds(0, nd - 1)], a_send.at[layer])
    drain(mz.at[pl.ds(0, (nz - 1) * 8)], m_send.at[0])
    drain(mrecv.at[pl.ds(0, 7)], m_send.at[1])


def body(
    pair,
    pair_mask,
    chain_ids,
    norm_gain,
    norm_shift,
    attn_proj,
    gate_shift,
    bias_proj,
    chain_scale,
    attn_out,
    trans_in,
    trans_out,
):
    n = pair.shape[1]
    nz = n // 64
    rows = 8 * nz
    vmem = pl.BlockSpec(memory_space=pltpu.VMEM)
    smem = pl.BlockSpec(memory_space=pltpu.SMEM)
    dma = pltpu.SemaphoreType.DMA
    return pl.pallas_call(
        functools.partial(kernel, nz),
        out_shape=jax.ShapeDtypeStruct(pair.shape, BF16),
        in_specs=[vmem] * 11 + [smem],
        out_specs=vmem,
        scratch_shapes=[
            pltpu.VMEM((8, n, C), F32),
            pltpu.VMEM((8 * n, C), F32),
            pltpu.VMEM((8, n, C), BF16),
            pltpu.VMEM((8, n, C), F32),
            pltpu.VMEM((8, n, C), BF16),
            pltpu.VMEM((8, n, 2 * C), BF16),
            pltpu.VMEM((8, n, C), F32),
            pltpu.VMEM((n // 128, 64, 128), F32),
            pltpu.VMEM((4 * rows, n), F32),
            pltpu.VMEM((8 * rows, C), BF16),
            pltpu.VMEM((2, 8, n), F32),
            pltpu.VMEM((n, 128), F32),
            pltpu.VMEM((128, n), F32),
            pltpu.VMEM((n, 128), F32),
            pltpu.VMEM((8, 8, 128), F32),
            pltpu.VMEM((2, 8, nz, 32, n), BF16),
            pltpu.VMEM((2, 8, nz, 64, C), BF16),
            pltpu.VMEM((2, 8 * nz, 64, C), BF16),
            dma((2,)),
            dma((2,)),
            dma((2,)),
            dma((2, 8)),
            dma((2,)),
            dma((2,)),
            dma((2,)),
            dma((2,)),
            dma,
        ],
        compiler_params=pltpu.CompilerParams(
            collective_id=0,
            has_side_effects=True,
            vmem_limit_bytes=56 * 1024 * 1024,
        ),
    )(
        pair,
        pair_mask,
        chain_ids.reshape(1, n),
        norm_gain,
        norm_shift,
        attn_proj,
        gate_shift,
        jnp.swapaxes(bias_proj, 1, 2),
        attn_out,
        trans_in,
        trans_out,
        chain_scale,
    )


def solution(mesh):
    in_specs = (
        P(("rep", "dap"), None, None),
        P(("rep", "dap"), None),
        P("rep"),
    ) + (P(),) * 9
    out_specs = P(("rep", "dap"), None, None)
    return jax.shard_map(body, mesh=mesh, in_specs=in_specs, out_specs=out_specs, check_vma=False)
```

time: 531 us -> 111 us (0.21)
  waiting for transfers between devices: 201 us -> 0 us
  matrix products: 159 us -> 0 us
  Pallas kernels: 0 us -> 107 us
  blocking collectives: 86.3 us -> 0 us
  local copies, waits for them, and re-layouts: 36.6 us -> 2.27 us
  other arithmetic: 31.1 us -> 0 us
  between operations: 13.7 us -> 0.01 us
    all_gather x2 -> x0, waiting for transfers between devices: 201 us -> none  [triangle(): lax.all_gather(planes.astype(jnp.bfloat16), 'dap', axis=1, tiled=True)]
    dot_general x53 -> x0, matrix products: 159 us -> none  [the longest x16 73.6 us: attend_block(): jnp.einsum('hjk,khd->jhd', weights, values, preferred_element_type=jnp.fl...]
    pallas_call x0 -> x1, Pallas kernels: none -> 107 us  [body(): pl.pallas_call(functools.partial(kernel, nz), out_shape=jax.ShapeDtypeStr...]
    all_to_all x3 -> x0, blocking collectives: 86.3 us -> none  [the longest x1 33.9 us: body(): lax.all_to_all(jnp.swapaxes(ending, 0, 1), 'dap', split_axis=0, concat_ax...]
    while x34 -> x0, local copies, waits for them, and re-layouts: 19.8 us -> none
    sub x16 -> x0, other arithmetic: 13 us -> none  [attend_block(): expd = jnp.exp(logits - top)]
    reduce_sum x6 -> x0, other arithmetic: 8.55 us -> none  [the longest x3 5.66 us: normalize(): var = jnp.mean(center * center, axis=-1, keepdims=True)]
    unnamed x24 -> x1, local copies, waits for them, and re-layouts: 9.7 us -> 2.27 us
  transfers between devices with their start and end apart: 2 -> 0, of which waited for: 2 -> 0; matrix products, arithmetic and copies ran while one was open for 3% -> 0% of each run, Pallas kernels for 0% -> 0%
where the time goes in v1:
time: 111 us; the launch traced here: 109 us
  Pallas kernels  107 us (96%)
  local copies, waits for them, and re-layouts  2.27 us (2%)
    pallas_call x1, Pallas kernels, body(): pl.pallas_call(functools.partial(kernel, nz), out_shape=jax.ShapeDtypeStr...  107 us
    unnamed x1, local copies, waits for them, and re-layouts  2.27 us

profile of v1, /device:TPU:2, one launch (start us, length us, event | category | flops | bytes accessed | tf_op | source)
XLA Modules:
  0.0 109.2 jit_solution(3130255688481004372)
XLA Ops:
  0.0 107.0 %shard_map.118 = bf16[8,512,128]{2,1,0:T(8,128)(2,1)} custom-call(bf16[8,512,128]{2,1,0:T(8,128)(2,1)} %pair.1, s32[8,512]{1,0:T(8,128)} %mask.1, s32[1,512]{1,0:T(1,128)} %bitcast.2, f32[3,128]{1,0:T(4,128)} %gain.1, f32[3,128]{1,0:T(4,128)} %shift.1, bf16[2,128,512]{2,1,0:T(8,128)(2,1)} %wp.1, f32[2,128]{1,0:T(2,128)} %gsh.1, bf16[2,4,128]{2,1,0:T(4,128)(2,1)} %bitcast.3, ...), custom_call_target="tpu_custom_call" | custom-call | tf_op jit(solution)/shard_map/pallas_call | solution.py:325
  107.0 2.3 %copy.14 = bf16[8,512,128]{2,1,0:T(8,128)(2,1)} copy(bf16[8,512,128]{2,1,0:T(8,128)(2,1)} %shard_map.118) | data formatting | bytes 2097152

commit v2 on v1

v2 whole, which is shorter than its diff:
```python
import functools

import jax
import jax.numpy as jnp
from jax import lax
from jax.experimental import pallas as pl
from jax.experimental.pallas import tpu as pltpu
from jax.sharding import PartitionSpec as P

C = 128
HEADS = 4
NZ = 8
ND = 64
N = 512
ROWS = 64
DX = (0, 0, 1, 3, 1, 3, 2, 2)
DY = (0, 1, 0, 0, 1, 1, 0, 1)
F32 = jnp.float32
BF16 = jnp.bfloat16
NT = (((1,), (1,)), ((), ()))


def layer_norm(x, gain, shift):
    mean = jnp.mean(x, axis=-1, keepdims=True)
    center = x - mean
    var = jnp.mean(center * center, axis=-1, keepdims=True)
    return center * lax.rsqrt(var + 1e-05) * gain + shift


def pick(t, table):
    value = jnp.int32(table[0])
    for index in range(1, len(table)):
        value = jnp.where(t == index, jnp.int32(table[index]), value)
    return value


def kernel(
    pair,
    mask,
    cid,
    gain,
    shift,
    wp,
    gsh,
    bp,
    wo,
    ti,
    to,
    scale,
    out,
    xs,
    xt,
    xn,
    q,
    k,
    vo,
    gate,
    bt,
    bx,
    gs,
    mrow,
    cidc,
    mz,
    mt,
    mrecv,
    planes,
    stage,
    recv,
    z_send,
    z_recv,
    p_send,
    p_recv,
    a_send,
    a_recv,
    m_send,
    m_recv,
    l_sem,
):
    me = lax.axis_index("dap")
    z = lax.rem(me, NZ)
    pm = lax.div(me, NZ)
    xx = lax.div(pm, 2)
    yy = lax.rem(pm, 2)

    def plane(dx, dy):
        return lax.rem(xx + dx, 4) * 2 + lax.rem(yy + dy, 2)

    def send(src, dst, send_sem, recv_sem, dest):
        pltpu.make_async_remote_copy(
            src_ref=src,
            dst_ref=dst,
            send_sem=send_sem,
            recv_sem=recv_sem,
            device_id={"dap": dest},
            device_id_type=pl.DeviceIdType.MESH,
        ).start()

    def drain(ref, sem):
        pltpu.make_async_copy(ref, ref, sem).wait()

    mz[...] = jnp.zeros_like(mz)
    barrier = pltpu.get_barrier_semaphore()

    def greet(d, carry):
        pl.semaphore_signal(
            barrier,
            inc=1,
            device_id={"dap": lax.rem(me + d, ND)},
            device_id_type=pl.DeviceIdType.MESH,
        )
        return carry

    lax.fori_loop(1, ND, greet, 0)
    mask_f = mask[...].astype(F32)
    mz_at = pl.ds(pl.multiple_of(yy * ROWS + z * 8, 8), 8)
    mz[mz_at, :] = mask_f
    lane_head = lax.div(lax.broadcasted_iota(jnp.int32, (1, 1, C), 2), 32)
    cid_row = cid[...].astype(F32)

    def lanes_of(index):
        return pl.ds(pl.multiple_of(index * 128, 128), 128)

    def norm(layer, at, x):
        xs[layer, :, lanes_of(at), :] = x.reshape(8, 128, C)
        xnv = layer_norm(x, gain[layer : layer + 1, :], shift[layer : layer + 1, :]).astype(BF16)
        xn[at] = xnv
        b = lax.dot_general(bp[layer], xnv, NT, preferred_element_type=F32)
        for r in range(8):
            bt[r * 8 : r * 8 + 4, :] = b[:, r * 128 : (r + 1) * 128]
        own = [bt[pl.ds(h, 8, stride=8), :] for h in range(HEADS)]
        planes[layer, pm, z, at] = jnp.concatenate(own, axis=0).astype(BF16)
        if layer == 0:
            return
        for d in range(1, NZ):
            ref = planes.at[layer, pm, z, at]
            send(ref, ref, z_send.at[layer], z_recv.at[layer, d], pm * NZ + lax.rem(z + d, NZ))

    def project(layer, at):
        f = jnp.dot(xn[at], wp[layer], preferred_element_type=F32)
        here = lanes_of(at)
        q[layer, :, here, :] = (f[:, :C] * (32 ** -0.5)).reshape(8, 128, C)
        k[layer, :, here, :] = f[:, C : 2 * C].astype(BF16).reshape(8, 128, C)
        vo[layer, :, here, :C] = f[:, 2 * C : 3 * C].astype(BF16).reshape(8, 128, C)
        g = jax.nn.sigmoid(f[:, 3 * C :] + gsh[layer : layer + 1, :])
        gate[layer, :, here, :] = g.reshape(8, 128, C)

    def arrive(layer, dx):
        source = lax.rem(xx + 4 - dx, 4)
        for yh in range(2):
            m = source * 2 + yh

            @pl.when(m == pm)
            def _():
                drain(recv.at[layer, pl.ds(0, NZ - 1)], a_recv.at[layer, m])

            @pl.when(m != pm)
            def _():
                drain(recv.at[layer, pl.ds(0, NZ)], a_recv.at[layer, m])

        for s in range(16):
            xt[s * 64 : (s + 1) * 64, :] = recv[layer, source * 16 + s].astype(F32)
        columns = [xt[pl.ds(c, 128, stride=8), :] for c in range(8)]
        if layer == 0:
            norm(1, source, jnp.concatenate(columns, axis=0))
        else:
            for i in range(8):
                out[i, lanes_of(source), :] = columns[i].astype(BF16)

    def first_norm(at, carry):
        norm(0, at, pair[:, lanes_of(at), :].astype(F32).reshape(1024, C))
        return carry

    lax.fori_loop(0, 4, first_norm, 0)
    pl.semaphore_wait(barrier, ND - 1)
    def share(ref, layer, m, offsets):
        for dx, dy in offsets:
            send(ref, ref, p_send.at[layer], p_recv.at[layer, m], plane(dx, dy) * NZ + z)

    def share_piece(layer, d):
        source = lax.rem(z + NZ - d, NZ)
        ref = planes.at[layer, pm, source]
        if d:
            drain(ref, z_recv.at[layer, d])
        share(ref, layer, pm, ((0, 1), (1, 0), (3, 0), (2, 0)))

    for d in (1, 7, 2, 6, 3, 5, 4):
        ref = planes.at[0, pm, z]
        send(ref, ref, z_send.at[0], z_recv.at[0, d], pm * NZ + lax.rem(z + d, NZ))
    share_piece(0, 0)
    project(0, 0)
    share_piece(0, 1)
    share_piece(0, 7)
    project(0, 1)
    share_piece(0, 2)
    share_piece(0, 6)
    project(0, 2)
    share_piece(0, 3)
    share_piece(0, 5)
    project(0, 3)
    cidc[...] = jnp.transpose(jnp.broadcast_to(cid_row, (128, N)))
    mrow[0] = (mask_f - 1.0) * 1e9
    ones = jnp.ones((N, C), BF16)
    for layer in range(2):
        for r in range(8):
            vo[layer, r, :, C:] = ones

    share_piece(0, 4)
    for d in range(1, NZ):
        ref = mz.at[mz_at, :]
        send(ref, ref, m_send.at[0], m_recv.at[0], pm * NZ + lax.rem(z + d, NZ))

    for layer in range(2):
        if layer == 1:
            for d in (0, 1, 7, 2, 6, 3, 5, 4):
                share_piece(1, d)

        def block(t, carry):
            m = plane(pick(t, DX), pick(t, DY))

            @pl.when((t > 0) & (t != 6))
            def _():
                drain(planes.at[layer, m], p_recv.at[layer, m])

            @pl.when(t == 1)
            def _():
                share(planes.at[layer, m], layer, m, ((1, 0), (3, 0)))

            @pl.when(t == 3)
            def _():
                far = plane(2, 0)
                ref = planes.at[layer, far]
                drain(ref, p_recv.at[layer, far])
                share(ref, layer, far, ((0, 1),))

            here = pl.ds(pl.multiple_of(m * ROWS, ROWS), ROWS)
            cb = cidc[here, :]
            for c in range(N // 128):
                lanes = slice(c * 128, (c + 1) * 128)
                same = jnp.where(cb == cid_row[:, lanes], 1.0, 0.0).reshape(NZ, 8, 128)
                b = planes[layer, m, :, c].astype(F32).reshape(NZ, HEADS, 8, 128)
                b = jnp.stack(
                    [b[:, h] + scale[layer, h] * same for h in range(HEADS)], axis=1
                )
                bx[:, lanes] = b.reshape(4 * ROWS, 128)

            for i in range(8):
                qi = q[layer, i, here, :].reshape(NZ, 8, C)
                qm = jnp.stack(
                    [jnp.where(lane_head == h, qi, 0.0) for h in range(HEADS)], axis=1
                )
                qm = qm.reshape(4 * ROWS, C).astype(BF16)
                s = lax.dot_general(qm, k[layer, i], NT, preferred_element_type=F32)
                s = s + bx[...] + mrow[layer, i : i + 1, :]
                top = jnp.max(s, axis=-1, keepdims=True)
                p = jnp.exp(s - top).astype(BF16)
                o = jnp.dot(p, vo[layer, i], preferred_element_type=F32)
                o = o.reshape(NZ, HEADS, 8, 2 * C)
                mixed, total = o[:, 0, :, :C], o[:, 0, :, C:]
                for h in range(1, HEADS):
                    mixed = jnp.where(lane_head == h, o[:, h, :, :C], mixed)
                    total = jnp.where(lane_head == h, o[:, h, :, C:], total)
                weighted = (mixed / total).reshape(ROWS, C) * gate[layer, i, here, :]
                gs[i * ROWS : (i + 1) * ROWS, :] = weighted.astype(BF16)

            y = jnp.dot(gs[...], wo[layer], preferred_element_type=F32)
            y = y + xs[layer, :, here, :].reshape(8 * ROWS, C)
            if layer == 1:
                y = y.astype(BF16).astype(F32)
                yn = layer_norm(y, gain[2:3, :], shift[2:3, :]).astype(BF16)
                inner = jnp.dot(yn, ti[...], preferred_element_type=F32)
                inner = jnp.maximum(inner, 0.0).astype(BF16)
                y = y + jnp.dot(inner, to[...], preferred_element_type=F32)
            y = y.reshape(8, NZ, 8, C)
            for zz in range(NZ):
                stage[layer, m, zz] = y[:, zz].reshape(64, C).astype(BF16)

            for d in range(NZ):
                zt = lax.rem(z + d, NZ)

                def go(zt=zt):
                    send(
                        stage.at[layer, m, zt],
                        recv.at[layer, me],
                        a_send.at[layer],
                        a_recv.at[layer, pm],
                        m * NZ + zt,
                    )

                if d == 0:
                    pl.when(t > 0)(go)

                    @pl.when(t == 0)
                    def _():
                        copy = pltpu.make_async_copy(
                            stage.at[layer, m, z], recv.at[layer, me], l_sem
                        )
                        copy.start()
                        copy.wait()
                else:
                    go()

            if layer == 0:

                @pl.when(t == 2)
                def _():
                    drain(mz.at[pl.ds(0, (NZ - 1) * 8)], m_recv.at[0])
                    mt[...] = jnp.transpose(mz[...])
                    for j in range(1, 8):
                        pt = plane(DX[j], DY[j])
                        src = mt.at[pl.ds(pl.multiple_of((pt * NZ + z) * 8, 8), 8), :]
                        send(src, mrecv.at[pm], m_send.at[1], m_recv.at[1], pt * NZ + z)
                    mrecv[pm] = mt[pl.ds(pl.multiple_of(me * 8, 8), 8), :]

            return carry

        lax.fori_loop(0, 8, block, 0)

        def late(index, carry):
            arrive(layer, pick(index, (0, 1, 3, 2)))
            if layer == 0:

                @pl.when(index > 0)
                def _():
                    project(1, lax.rem(xx + 4 - pick(index, (0, 0, 1, 3)), 4))

            return carry

        lax.fori_loop(0, 4, late, 0)
        if layer == 0:
            project(1, lax.rem(xx + 2, 4))
        if layer == 0:
            drain(mrecv.at[pl.ds(0, 7)], m_recv.at[1])
            parts = [mrecv[2 * c] + mrecv[2 * c + 1] for c in range(N // 128)]
            mrow[1] = (jnp.concatenate(parts, axis=1) - 1.0) * 1e9

    for layer in range(2):
        drain(planes.at[layer, 0, pl.ds(0, NZ - 1)], z_send.at[layer])
        drain(planes.at[layer, pl.ds(0, 7)], p_send.at[layer])
        drain(recv.at[layer, pl.ds(0, ND - 1)], a_send.at[layer])
    drain(mz.at[pl.ds(0, (NZ - 1) * 8)], m_send.at[0])
    drain(mrecv.at[pl.ds(0, 7)], m_send.at[1])


def body(
    pair,
    pair_mask,
    chain_ids,
    norm_gain,
    norm_shift,
    attn_proj,
    gate_shift,
    bias_proj,
    chain_scale,
    attn_out,
    trans_in,
    trans_out,
):
    vmem = pl.BlockSpec(memory_space=pltpu.VMEM)
    smem = pl.BlockSpec(memory_space=pltpu.SMEM)
    dma = pltpu.SemaphoreType.DMA
    return pl.pallas_call(
        kernel,
        out_shape=jax.ShapeDtypeStruct(pair.shape, BF16),
        in_specs=[vmem] * 11 + [smem],
        out_specs=vmem,
        scratch_shapes=[
            pltpu.VMEM((2, 8, N, C), F32),
            pltpu.VMEM((1024, C), F32),
            pltpu.VMEM((4, 1024, C), BF16),
            pltpu.VMEM((2, 8, N, C), F32),
            pltpu.VMEM((2, 8, N, C), BF16),
            pltpu.VMEM((2, 8, N, 2 * C), BF16),
            pltpu.VMEM((2, 8, N, C), F32),
            pltpu.VMEM((64, 128), F32),
            pltpu.VMEM((4 * ROWS, N), F32),
            pltpu.VMEM((8 * ROWS, C), BF16),
            pltpu.VMEM((2, 8, N), F32),
            pltpu.VMEM((N, 128), F32),
            pltpu.VMEM((128, N), F32),
            pltpu.VMEM((N, 128), F32),
            pltpu.VMEM((8, 8, 128), F32),
            pltpu.VMEM((2, 8, NZ, 4, 32, 128), BF16),
            pltpu.VMEM((2, 8, NZ, 64, C), BF16),
            pltpu.VMEM((2, ND, 64, C), BF16),
            dma((2,)),
            dma((2, NZ)),
            dma((2,)),
            dma((2, 8)),
            dma((2,)),
            dma((2, 8)),
            dma((2,)),
            dma((2,)),
            dma,
        ],
        compiler_params=pltpu.CompilerParams(
            collective_id=0,
            has_side_effects=True,
            vmem_limit_bytes=56 * 1024 * 1024,
        ),
    )(
        pair,
        pair_mask,
        chain_ids.reshape(1, N),
        norm_gain,
        norm_shift,
        attn_proj,
        gate_shift,
        jnp.swapaxes(bias_proj, 1, 2),
        attn_out,
        trans_in,
        trans_out,
        chain_scale,
    )


def solution(mesh):
    in_specs = (
        P(("rep", "dap"), None, None),
        P(("rep", "dap"), None),
        P("rep"),
    ) + (P(),) * 9
    out_specs = P(("rep", "dap"), None, None)
    return jax.shard_map(body, mesh=mesh, in_specs=in_specs, out_specs=out_specs, check_vma=False)
```

time: 111 us -> 95.6 us (0.86); the launches traced: 109 us -> 95.5 us
  Pallas kernels: 107 us -> 93.2 us
    pallas_call x1, Pallas kernels: 107 us -> 93.2 us  [body(): pl.pallas_call(kernel, out_shape=jax.ShapeDtypeStruct(pair.shape, BF16),...]
where the time goes in v2:
time: 95.6 us; the launch traced here: 95.5 us
  Pallas kernels  93.2 us (97%)
  local copies, waits for them, and re-layouts  2.27 us (2%)
    pallas_call x1, Pallas kernels, body(): pl.pallas_call(kernel, out_shape=jax.ShapeDtypeStruct(pair.shape, BF16),...  93.2 us
    unnamed x1, local copies, waits for them, and re-layouts  2.27 us

profile of v2, /device:TPU:2, one launch (start us, length us, event | category | flops | bytes accessed | tf_op | source)
XLA Modules:
  0.0 95.5 jit_solution(5841026715093237295)
XLA Ops:
  0.0 93.2 %shard_map.118 = bf16[8,512,128]{2,1,0:T(8,128)(2,1)} custom-call(bf16[8,512,128]{2,1,0:T(8,128)(2,1)} %pair.1, s32[8,512]{1,0:T(8,128)} %mask.1, s32[1,512]{1,0:T(1,128)} %bitcast.2, f32[3,128]{1,0:T(4,128)} %gain.1, f32[3,128]{1,0:T(4,128)} %shift.1, bf16[2,128,512]{2,1,0:T(8,128)(2,1)} %wp.1, f32[2,128]{1,0:T(2,128)} %gsh.1, bf16[2,4,128]{2,1,0:T(4,128)(2,1)} %bitcast.3, ...), custom_call_target="tpu_custom_call" | custom-call | tf_op jit(solution)/shard_map/pallas_call | solution.py:361
  93.2 2.3 %copy.14 = bf16[8,512,128]{2,1,0:T(8,128)(2,1)} copy(bf16[8,512,128]{2,1,0:T(8,128)(2,1)} %shard_map.118) | data formatting | bytes 2097152

commit v3 on v2

--- a/solution.py
+++ b/solution.py
@@ -70,6 +70,7 @@
     z_recv,
     p_send,
     p_recv,
+    f_recv,
     a_send,
     a_recv,
     m_send,
@@ -134,6 +135,7 @@
         for d in range(1, NZ):
             ref = planes.at[layer, pm, z, at]
             send(ref, ref, z_send.at[layer], z_recv.at[layer, d], pm * NZ + lax.rem(z + d, NZ))
+        send(ref, ref, p_send.at[layer], f_recv, plane(2, 0) * NZ + z)
 
     def project(layer, at):
         f = jnp.dot(xn[at], wp[layer], preferred_element_type=F32)
@@ -181,7 +183,15 @@
         ref = planes.at[layer, pm, source]
         if d:
             drain(ref, z_recv.at[layer, d])
-        share(ref, layer, pm, ((0, 1), (1, 0), (3, 0), (2, 0)))
+        near = ((0, 1), (1, 0), (3, 0))
+        share(ref, layer, pm, near + ((2, 0),) if layer == 0 else near)
+
+    def spread_far(layer):
+        far = plane(2, 0)
+        ref = planes.at[layer, far, z]
+        drain(ref, f_recv)
+        for d in (1, 7, 2, 6, 3, 5, 4):
+            send(ref, ref, p_send.at[layer], p_recv.at[layer, far], pm * NZ + lax.rem(z + d, NZ))
 
     for d in (1, 7, 2, 6, 3, 5, 4):
         ref = planes.at[0, pm, z]
@@ -211,6 +221,7 @@
 
     for layer in range(2):
         if layer == 1:
+            spread_far(1)
             for d in (0, 1, 7, 2, 6, 3, 5, 4):
                 share_piece(1, d)
 
@@ -228,9 +239,9 @@
             @pl.when(t == 3)
             def _():
                 far = plane(2, 0)
-                ref = planes.at[layer, far]
-                drain(ref, p_recv.at[layer, far])
-                share(ref, layer, far, ((0, 1),))
+                pieces = NZ if layer == 0 else NZ - 1
+                drain(planes.at[layer, far, pl.ds(0, pieces)], p_recv.at[layer, far])
+                share(planes.at[layer, far], layer, far, ((0, 1),))
 
             here = pl.ds(pl.multiple_of(m * ROWS, ROWS), ROWS)
             cb = cidc[here, :]
@@ -386,6 +397,7 @@
             dma((2, NZ)),
             dma((2,)),
             dma((2, 8)),
+            dma,
             dma((2,)),
             dma((2, 8)),
             dma((2,)),

time: 95.6 us -> 92.7 us (0.970)
  Pallas kernels: 93.2 us -> 90.2 us
    pallas_call x1, Pallas kernels: 93.2 us -> 90.2 us  [body(): pl.pallas_call(kernel, out_shape=jax.ShapeDtypeStruct(pair.shape, BF16),...]
where the time goes in v3:
time: 92.7 us; the launch traced here: 92.5 us
  Pallas kernels  90.2 us (97%)
  local copies, waits for them, and re-layouts  2.27 us (2%)
    pallas_call x1, Pallas kernels, body(): pl.pallas_call(kernel, out_shape=jax.ShapeDtypeStruct(pair.shape, BF16),...  90.2 us
    unnamed x1, local copies, waits for them, and re-layouts  2.27 us

profile of v3, /device:TPU:2, one launch (start us, length us, event | category | flops | bytes accessed | tf_op | source)
XLA Modules:
  0.0 92.5 jit_solution(15220476630893898106)
XLA Ops:
  0.0 90.2 %shard_map.118 = bf16[8,512,128]{2,1,0:T(8,128)(2,1)} custom-call(bf16[8,512,128]{2,1,0:T(8,128)(2,1)} %pair.1, s32[8,512]{1,0:T(8,128)} %mask.1, s32[1,512]{1,0:T(1,128)} %bitcast.2, f32[3,128]{1,0:T(4,128)} %gain.1, f32[3,128]{1,0:T(4,128)} %shift.1, bf16[2,128,512]{2,1,0:T(8,128)(2,1)} %wp.1, f32[2,128]{1,0:T(2,128)} %gsh.1, bf16[2,4,128]{2,1,0:T(4,128)(2,1)} %bitcast.3, ...), custom_call_target="tpu_custom_call" | custom-call | tf_op jit(solution)/shard_map/pallas_call | solution.py:372
  90.3 2.3 %copy.14 = bf16[8,512,128]{2,1,0:T(8,128)(2,1)} copy(bf16[8,512,128]{2,1,0:T(8,128)(2,1)} %shard_map.118) | data formatting | bytes 2097152

commit v4 on v3

--- a/solution.py
+++ b/solution.py
@@ -35,19 +35,25 @@
 
 
 def kernel(
-    pair,
+    pair_in,
     mask,
     cid,
     gain,
     shift,
-    wp,
+    wp_in,
     gsh,
     bp,
+    wo_in,
+    ti_in,
+    to_in,
+    scale,
+    out,
+    done,
+    pair,
+    wp,
     wo,
     ti,
     to,
-    scale,
-    out,
     xs,
     xt,
     xn,
@@ -76,6 +82,8 @@
     m_send,
     m_recv,
     l_sem,
+    i_sem,
+    o_sem,
 ):
     me = lax.axis_index("dap")
     z = lax.rem(me, NZ)
@@ -99,6 +107,22 @@
     def drain(ref, sem):
         pltpu.make_async_copy(ref, ref, sem).wait()
 
+    def fetch(at):
+        here = pl.ds(pl.multiple_of(at * 128, 128), 128)
+        return pltpu.make_async_copy(
+            pair_in.at[:, here, :], pair.at[:, here, :], i_sem.at[at]
+        )
+
+    fetched = [
+        pltpu.make_async_copy(source, target, i_sem.at[4 + index])
+        for index, (source, target) in enumerate(
+            ((wp_in, wp), (wo_in, wo), (ti_in, ti), (to_in, to))
+        )
+    ]
+    for at in range(4):
+        fetch(at).start()
+    for copy in fetched:
+        copy.start()
     mz[...] = jnp.zeros_like(mz)
     barrier = pltpu.get_barrier_semaphore()
 
@@ -146,6 +170,10 @@
         g = jax.nn.sigmoid(f[:, 3 * C :] + gsh[layer : layer + 1, :])
         gate[layer, :, here, :] = g.reshape(8, 128, C)
 
+    def deliver(at):
+        here = lanes_of(at)
+        return pltpu.make_async_copy(done.at[:, here, :], out.at[:, here, :], o_sem.at[at])
+
     def arrive(layer, dx):
         source = lax.rem(xx + 4 - dx, 4)
         for yh in range(2):
@@ -166,9 +194,11 @@
             norm(1, source, jnp.concatenate(columns, axis=0))
         else:
             for i in range(8):
-                out[i, lanes_of(source), :] = columns[i].astype(BF16)
+                done[i, lanes_of(source), :] = columns[i].astype(BF16)
+            deliver(source).start()
 
     def first_norm(at, carry):
+        fetch(at).wait()
         norm(0, at, pair[:, lanes_of(at), :].astype(F32).reshape(1024, C))
         return carry
 
@@ -197,6 +227,8 @@
         ref = planes.at[0, pm, z]
         send(ref, ref, z_send.at[0], z_recv.at[0, d], pm * NZ + lax.rem(z + d, NZ))
     share_piece(0, 0)
+    for copy in fetched:
+        copy.wait()
     project(0, 0)
     share_piece(0, 1)
     share_piece(0, 7)
@@ -344,6 +376,8 @@
             parts = [mrecv[2 * c] + mrecv[2 * c + 1] for c in range(N // 128)]
             mrow[1] = (jnp.concatenate(parts, axis=1) - 1.0) * 1e9
 
+    for at in range(4):
+        deliver(at).wait()
     for layer in range(2):
         drain(planes.at[layer, 0, pl.ds(0, NZ - 1)], z_send.at[layer])
         drain(planes.at[layer, pl.ds(0, 7)], p_send.at[layer])
@@ -368,13 +402,20 @@
 ):
     vmem = pl.BlockSpec(memory_space=pltpu.VMEM)
     smem = pl.BlockSpec(memory_space=pltpu.SMEM)
+    anywhere = pl.BlockSpec(memory_space=pl.ANY)
     dma = pltpu.SemaphoreType.DMA
     return pl.pallas_call(
         kernel,
         out_shape=jax.ShapeDtypeStruct(pair.shape, BF16),
-        in_specs=[vmem] * 11 + [smem],
-        out_specs=vmem,
+        in_specs=[anywhere] + [vmem] * 4 + [anywhere] + [vmem] * 2 + [anywhere] * 3 + [smem],
+        out_specs=anywhere,
         scratch_shapes=[
+            pltpu.VMEM((8, N, C), BF16),
+            pltpu.VMEM((8, N, C), BF16),
+            pltpu.VMEM((2, C, 4 * C), BF16),
+            pltpu.VMEM((2, C, C), BF16),
+            pltpu.VMEM((C, 4 * C), BF16),
+            pltpu.VMEM((4 * C, C), BF16),
             pltpu.VMEM((2, 8, N, C), F32),
             pltpu.VMEM((1024, C), F32),
             pltpu.VMEM((4, 1024, C), BF16),
@@ -403,6 +444,8 @@
             dma((2,)),
             dma((2,)),
             dma,
+            dma((8,)),
+            dma((4,)),
         ],
         compiler_params=pltpu.CompilerParams(
             collective_id=0,

time: 92.7 us -> 92 us (level)
  no operation moved by 1% of the time
where the time goes in v4:
time: 92 us; the launch traced here: 91.7 us
  Pallas kernels  89.5 us (97%)
  local copies, waits for them, and re-layouts  2.27 us (2%)
    pallas_call x1, Pallas kernels, body(): pl.pallas_call(kernel, out_shape=jax.ShapeDtypeStruct(pair.shape, BF16),...  89.5 us
    unnamed x1, local copies, waits for them, and re-layouts  2.27 us

profile of v4, /device:TPU:2, one launch (start us, length us, event | category | flops | bytes accessed | tf_op | source)
XLA Modules:
  0.0 91.7 jit_solution(2925507327299350861)
XLA Ops:
  0.0 89.5 %shard_map.118 = bf16[8,512,128]{2,1,0:T(8,128)(2,1)} custom-call(bf16[8,512,128]{2,1,0:T(8,128)(2,1)} %pair_in.1, s32[8,512]{1,0:T(8,128)} %mask.1, s32[1,512]{1,0:T(1,128)} %bitcast.2, f32[3,128]{1,0:T(4,128)} %gain.1, f32[3,128]{1,0:T(4,128)} %shift.1, bf16[2,128,512]{2,1,0:T(8,128)(2,1)} %wp_in.1, f32[2,128]{1,0:T(2,128)} %gsh.1, ...), custom_call_target="tpu_custom_call" | custom-call | tf_op jit(solution)/shard_map/pallas_call | solution.py:407
  89.5 2.3 %copy.14 = bf16[8,512,128]{2,1,0:T(8,128)(2,1)} copy(bf16[8,512,128]{2,1,0:T(8,128)(2,1)} %shard_map.118) | data formatting | bytes 2097152

commit v5 on v4

--- a/solution.py
+++ b/solution.py
@@ -318,7 +318,7 @@
                 stage[layer, m, zz] = y[:, zz].reshape(64, C).astype(BF16)
 
             for d in range(NZ):
-                zt = lax.rem(z + d, NZ)
+                zt = lax.rem(z + (0, 4, 3, 5, 2, 6, 1, 7)[d], NZ)
 
                 def go(zt=zt):
                     send(

time: 92 us -> 90.5 us (0.984)
  Pallas kernels: 89.5 us -> 88.1 us
    pallas_call x1, Pallas kernels: 89.5 us -> 88.1 us  [body(): pl.pallas_call(kernel, out_shape=jax.ShapeDtypeStruct(pair.shape, BF16),...]
where the time goes in v5:
time: 90.5 us; the launch traced here: 90.4 us
  Pallas kernels  88.1 us (97%)
  local copies, waits for them, and re-layouts  2.27 us (3%)
    pallas_call x1, Pallas kernels, body(): pl.pallas_call(kernel, out_shape=jax.ShapeDtypeStruct(pair.shape, BF16),...  88.1 us
    unnamed x1, local copies, waits for them, and re-layouts  2.27 us

profile of v5, /device:TPU:2, one launch (start us, length us, event | category | flops | bytes accessed | tf_op | source)
XLA Modules:
  0.0 90.4 jit_solution(4928701450004542851)
XLA Ops:
  0.0 88.1 %shard_map.118 = bf16[8,512,128]{2,1,0:T(8,128)(2,1)} custom-call(bf16[8,512,128]{2,1,0:T(8,128)(2,1)} %pair_in.1, s32[8,512]{1,0:T(8,128)} %mask.1, s32[1,512]{1,0:T(1,128)} %bitcast.2, f32[3,128]{1,0:T(4,128)} %gain.1, f32[3,128]{1,0:T(4,128)} %shift.1, bf16[2,128,512]{2,1,0:T(8,128)(2,1)} %wp_in.1, f32[2,128]{1,0:T(2,128)} %gsh.1, ...), custom_call_target="tpu_custom_call" | custom-call | tf_op jit(solution)/shard_map/pallas_call | solution.py:407
  88.1 2.3 %copy.14 = bf16[8,512,128]{2,1,0:T(8,128)(2,1)} copy(bf16[8,512,128]{2,1,0:T(8,128)(2,1)} %shard_map.118) | data formatting | bytes 2097152
